TPU v7x, 32 devices: a whole 2x2x4 slice. The times are simulated.
32 devices in a mesh: dp: 4 (over z), sq: 8 (over y, x, core).
Axes of the slice: x: 2, y: 2, z: 4, core: 2. Of those that a mesh axis runs over, the one named last changes fastest.
Arguments:
- frames: bfloat16 [4, 1024, 1024], P('dp', 'sq'), may hold values from -6 to 6
- norm1_gain: float32 [1024], replicated, may hold values from 0.5 to 1.5
- w_qkv: bfloat16 [1024, 3072], replicated, may hold values from -0.1875 to 0.1875
- w_out: bfloat16 [1024, 1024], replicated, may hold values from -0.75 to 0.75
- norm2_gain: float32 [1024], replicated, may hold values from 0.5 to 1.5
- w_up: bfloat16 [1024, 4096], replicated, may hold values from -0.1875 to 0.1875
- w_down: bfloat16 [4096, 1024], replicated, may hold values from -0.09375 to 0.09375
- lengths: int32 [4, 8], P('dp'), may hold values from 1 to 896, as said below
- cotangent: bfloat16 [4, 1024, 1024], P('dp', 'sq'), may hold values from -6 to 6
Outputs:
- out: bfloat16 [4, 1024, 1024], P('dp', 'sq')
- d_in: float32 [4, 1024, 1024], P('dp', 'sq')
- g_norm1: float32 [1024], P('sq')
- g_qkv: float32 [1024, 3072], P('sq')
- g_out: float32 [1024, 1024], P('sq')
- g_norm2: float32 [1024], P('sq')
- g_up: float32 [1024, 4096], P('sq')
- g_down: float32 [4096, 1024], P('sq')
Inputs may be any that keep to these rules, and one draw needn't show every extreme that they name: Each row's lengths sum to 1024. In each row exactly one item has 896 frames and is neither the first nor the last item of the row; the other items share the remaining 128 frames.
All inputs are finite; a program needn't handle non-finite values.
Results may differ from a plain program's by a relative error of at most 0.025.
Values may be sent and summed in bfloat16 or wider, within the bound.
A program may use at most 256 MiB of HBM per device.

v0:
```python
import jax
import jax.numpy as jnp
from jax import lax
from jax.sharding import PartitionSpec as P

HEADS = 16
HEAD_DIM = 64
EPSILON = 1e-05
NEG_FILL = -1000000000.0
START_MAX = -1e30


def norm_scaled(values, gain):
    return values * lax.rsqrt(jnp.mean(values * values, axis=-1, keepdims=True) + EPSILON) * gain


def segment_ids(positions, item_ends):
    return jnp.sum((positions[None, :, None] >= item_ends[:, None, :]).astype(jnp.int32), axis=2)


def visible(query_pos, query_seg, key_pos, key_seg):
    return (key_pos[None, None, :] <= query_pos[None, :, None]) & (
        key_seg[:, None, :] == query_seg[:, :, None]
    )


def block_size(count, limit):
    for candidate in range(min(count, limit), 0, -1):
        if count % candidate == 0:
            return candidate
    return count


def over_blocks(carry, arrays, start, step_fn, limit):
    count = arrays[0].shape[1]
    size = block_size(count, limit)
    number = count // size
    if number == 1:
        return step_fn(carry, arrays, start)
    stacked = tuple(
        (
            jnp.swapaxes(member.reshape((member.shape[0], number, size) + member.shape[2:]), 0, 1)
            for member in arrays
        )
    )

    def turn(state, item):
        offset, pieces = item
        return (step_fn(state, pieces, start + offset * size), None)

    offsets = jnp.arange(number, dtype=jnp.int32)
    return lax.scan(turn, carry, (offsets, stacked))[0]


def contract_rows(left, right):
    return lax.dot_general(
        left, right, (((0,), (0,)), ((), ())), preferred_element_type=jnp.float32
    )


def times_transpose(left, right):
    return lax.dot_general(
        left, right, (((1,), (1,)), ((), ())), preferred_element_type=jnp.float32
    )


def heads_flat(values, batch, rows, width):
    return values.transpose(0, 2, 1, 3).reshape(batch * rows, width)


def shards(frames, norm1_gain, w_qkv, w_out, norm2_gain, w_up, w_down, lengths, cotangent):
    batch = frames.shape[0]
    rows = frames.shape[1]
    width = frames.shape[2]
    factor = HEAD_DIM ** (-0.5)
    first = lax.axis_index("sq") * rows
    query_pos = first + jnp.arange(rows, dtype=jnp.int32)
    item_ends = jnp.cumsum(lengths, axis=1)
    query_seg = segment_ids(query_pos, item_ends)
    frames_own = frames.reshape(batch * rows, width).astype(jnp.float32)
    hidden1, norm1_pull = jax.vjp(norm_scaled, frames_own, norm1_gain)
    hidden1_low = hidden1.astype(jnp.bfloat16)
    mixed = jnp.dot(hidden1_low, w_qkv, preferred_element_type=jnp.float32).astype(jnp.bfloat16)
    query_rows = mixed[:, :width].reshape(batch, rows, width)
    key_rows = mixed[:, width : 2 * width].reshape(batch, rows, width)
    value_rows = mixed[:, 2 * width :].reshape(batch, rows, width)
    queries = query_rows.reshape(batch, rows, HEADS, HEAD_DIM)
    keys_own = key_rows.reshape(batch, rows, HEADS, HEAD_DIM)
    values_own = value_rows.reshape(batch, rows, HEADS, HEAD_DIM)

    def forward_step(carry, pieces, start):
        key_piece, value_piece = pieces
        count = key_piece.shape[1]
        key_pos = start + jnp.arange(count, dtype=jnp.int32)
        key_seg = segment_ids(key_pos, item_ends)

        def forward_work(state):
            running_max, running_sum, accum = state
            keys_block = key_piece.reshape(batch, count, HEADS, HEAD_DIM)
            values_block = value_piece.reshape(batch, count, HEADS, HEAD_DIM)
            scores = (
                jnp.einsum(
                    "rqhd,rkhd->rhqk", queries, keys_block, preferred_element_type=jnp.float32
                )
                * factor
            )
            mask = visible(query_pos, query_seg, key_pos, key_seg)[:, None]
            scores = jnp.where(mask, scores, NEG_FILL)
            new_max = jnp.maximum(running_max, jnp.max(scores, axis=-1))
            weights = jnp.where(mask, jnp.exp(scores - new_max[..., None]), 0.0)
            decay = jnp.exp(running_max - new_max)
            new_sum = decay * running_sum + jnp.sum(weights, axis=-1)
            update = jnp.einsum(
                "rhqk,rkhd->rhqd",
                weights.astype(jnp.bfloat16),
                values_block,
                preferred_element_type=jnp.float32,
            )
            return (new_max, new_sum, decay[..., None] * accum + update)

        return lax.cond(start <= query_pos[-1], forward_work, lambda state: state, carry)

    start_state = (
        jnp.full((batch, HEADS, rows), START_MAX, jnp.float32),
        jnp.zeros((batch, HEADS, rows), jnp.float32),
        jnp.zeros((batch, HEADS, rows, HEAD_DIM), jnp.float32),
    )
    final_max, final_sum, accum = over_blocks(
        start_state,
        (
            lax.all_gather(key_rows, "sq", axis=1, tiled=True),
            lax.all_gather(value_rows, "sq", axis=1, tiled=True),
        ),
        jnp.int32(0),
        forward_step,
        512,
    )
    attended = heads_flat(accum / final_sum[..., None], batch, rows, width)
    log_total = final_max + jnp.log(final_sum)
    attended_low = attended.astype(jnp.bfloat16)
    middle = frames_own + jnp.dot(attended_low, w_out, preferred_element_type=jnp.float32)
    hidden2, norm2_pull = jax.vjp(norm_scaled, middle, norm2_gain)
    hidden2_low = hidden2.astype(jnp.bfloat16)
    upward = jnp.dot(hidden2_low, w_up, preferred_element_type=jnp.float32)
    active, gelu_pull = jax.vjp(jax.nn.gelu, upward)
    active_low = active.astype(jnp.bfloat16)
    result = middle + jnp.dot(active_low, w_down, preferred_element_type=jnp.float32)
    grad_top = cotangent.reshape(batch * rows, width).astype(jnp.float32)
    grad_branch = grad_top.astype(jnp.bfloat16)
    grad_down = contract_rows(active_low, grad_branch)
    grad_active = times_transpose(grad_branch, w_down)
    grad_upward = gelu_pull(grad_active)[0].astype(jnp.bfloat16)
    grad_up = contract_rows(hidden2_low, grad_upward)
    grad_hidden2 = times_transpose(grad_upward, w_up)
    grad_middle_part, grad_gain2 = norm2_pull(grad_hidden2)
    grad_middle = grad_top + grad_middle_part
    grad_attn = grad_middle.astype(jnp.bfloat16)
    grad_outproj = contract_rows(attended_low, grad_attn)
    grad_attended = times_transpose(grad_attn, w_out).astype(jnp.bfloat16)
    grad_rows_own = grad_attended.reshape(batch, rows, width)
    grad_heads = grad_attended.reshape(batch, rows, HEADS, HEAD_DIM)
    delta_rows = jnp.sum(
        (grad_attended.astype(jnp.float32) * attended).reshape(batch, rows, HEADS, HEAD_DIM), axis=3
    )
    delta = delta_rows.transpose(0, 2, 1)

    def query_step(carry, pieces, start):
        key_piece, value_piece = pieces
        count = key_piece.shape[1]
        key_pos = start + jnp.arange(count, dtype=jnp.int32)
        key_seg = segment_ids(key_pos, item_ends)

        def query_work(grad_query):
            keys_block = key_piece.reshape(batch, count, HEADS, HEAD_DIM)
            values_block = value_piece.reshape(batch, count, HEADS, HEAD_DIM)
            scores = (
                jnp.einsum(
                    "rqhd,rkhd->rhqk", queries, keys_block, preferred_element_type=jnp.float32
                )
                * factor
            )
            mask = visible(query_pos, query_seg, key_pos, key_seg)[:, None]
            shares = jnp.where(mask, jnp.exp(scores - log_total[..., None]), 0.0)
            grad_shares = jnp.einsum(
                "rqhd,rkhd->rhqk", grad_heads, values_block, preferred_element_type=jnp.float32
            )
            grad_scores = (shares * (grad_shares - delta[..., None])).astype(jnp.bfloat16)
            return grad_query + jnp.einsum(
                "rhqk,rkhd->rhqd", grad_scores, keys_block, preferred_element_type=jnp.float32
            )

        return lax.cond(start <= query_pos[-1], query_work, lambda state: state, carry)

    zero_query = jnp.zeros((batch, HEADS, rows, HEAD_DIM), jnp.float32)
    grad_query = over_blocks(
        zero_query,
        (
            lax.all_gather(key_rows, "sq", axis=1, tiled=True),
            lax.all_gather(value_rows, "sq", axis=1, tiled=True),
        ),
        jnp.int32(0),
        query_step,
        512,
    )

    def key_step(carry, pieces, start):
        query_piece, grad_piece, total_piece, delta_piece = pieces
        count = query_piece.shape[1]
        remote_pos = start + jnp.arange(count, dtype=jnp.int32)
        remote_seg = segment_ids(remote_pos, item_ends)

        def key_work(state):
            grad_key, grad_value = state
            remote_queries = query_piece.reshape(batch, count, HEADS, HEAD_DIM)
            remote_grads = grad_piece.reshape(batch, count, HEADS, HEAD_DIM)
            scores = (
                jnp.einsum(
                    "rqhd,rkhd->rhqk", remote_queries, keys_own, preferred_element_type=jnp.float32
                )
                * factor
            )
            mask = visible(remote_pos, remote_seg, query_pos, query_seg)[:, None]
            shares = jnp.where(
                mask, jnp.exp(scores - total_piece.transpose(0, 2, 1)[..., None]), 0.0
            )
            grad_value = grad_value + jnp.einsum(
                "rhqk,rqhd->rhkd",
                shares.astype(jnp.bfloat16),
                remote_grads,
                preferred_element_type=jnp.float32,
            )
            grad_shares = jnp.einsum(
                "rqhd,rkhd->rhqk", remote_grads, values_own, preferred_element_type=jnp.float32
            )
            grad_scores = (
                shares * (grad_shares - delta_piece.transpose(0, 2, 1)[..., None])
            ).astype(jnp.bfloat16)
            grad_key = grad_key + jnp.einsum(
                "rhqk,rqhd->rhkd", grad_scores, remote_queries, preferred_element_type=jnp.float32
            )
            return (grad_key, grad_value)

        return lax.cond(start + count - 1 >= first, key_work, lambda state: state, carry)

    grad_key, grad_value = over_blocks(
        (zero_query, zero_query),
        (
            lax.all_gather(query_rows, "sq", axis=1, tiled=True),
            lax.all_gather(grad_rows_own, "sq", axis=1, tiled=True),
            lax.all_gather(
                log_total.transpose(0, 2, 1).astype(jnp.bfloat16), "sq", axis=1, tiled=True
            ).astype(jnp.float32),
            lax.all_gather(delta_rows.astype(jnp.bfloat16), "sq", axis=1, tiled=True).astype(
                jnp.float32
            ),
        ),
        jnp.int32(0),
        key_step,
        512,
    )
    grad_mixed = jnp.concatenate(
        [
            heads_flat(grad_query * factor, batch, rows, width),
            heads_flat(grad_key * factor, batch, rows, width),
            heads_flat(grad_value, batch, rows, width),
        ],
        axis=1,
    ).astype(jnp.bfloat16)
    grad_qkv = contract_rows(hidden1_low, grad_mixed)
    grad_hidden1 = times_transpose(grad_mixed, w_qkv)
    grad_frames_part, grad_gain1 = norm1_pull(grad_hidden1)
    grad_frames = (grad_middle + grad_frames_part).reshape(batch, rows, width)
    result_rows = result.astype(jnp.bfloat16).reshape(batch, rows, width)
    shares_sq = (
        lax.psum_scatter(grad_gain1, "sq", scatter_dimension=0, tiled=True),
        lax.psum_scatter(grad_qkv, "sq", scatter_dimension=0, tiled=True),
        lax.psum_scatter(grad_outproj, "sq", scatter_dimension=0, tiled=True),
        lax.psum_scatter(grad_gain2, "sq", scatter_dimension=0, tiled=True),
        lax.psum_scatter(grad_up, "sq", scatter_dimension=0, tiled=True),
        lax.psum_scatter(grad_down, "sq", scatter_dimension=0, tiled=True),
    )
    totals = (
        lax.psum(shares_sq[0].astype(jnp.bfloat16), "dp").astype(jnp.float32),
        lax.psum(shares_sq[1].astype(jnp.bfloat16), "dp").astype(jnp.float32),
        lax.psum(shares_sq[2].astype(jnp.bfloat16), "dp").astype(jnp.float32),
        lax.psum(shares_sq[3].astype(jnp.bfloat16), "dp").astype(jnp.float32),
        lax.psum(shares_sq[4].astype(jnp.bfloat16), "dp").astype(jnp.float32),
        lax.psum(shares_sq[5].astype(jnp.bfloat16), "dp").astype(jnp.float32),
    )
    return (
        result_rows,
        grad_frames,
        totals[0],
        totals[1],
        totals[2],
        totals[3],
        totals[4],
        totals[5],
    )


def solution(mesh):
    return jax.shard_map(
        shards,
        mesh=mesh,
        in_specs=(
            P("dp", "sq", None),
            P(),
            P(),
            P(),
            P(),
            P(),
            P(),
            P("dp", None),
            P("dp", "sq", None),
        ),
        out_specs=(
            P("dp", "sq", None),
            P("dp", "sq", None),
            P("sq"),
            P("sq", None),
            P("sq", None),
            P("sq"),
            P("sq", None),
            P("sq", None),
        ),
        check_vma=False,
    )
```

profile of v0, /device:TPU:0, one launch (start us, length us, event | category | flops | bytes accessed | tf_op | source)
XLA Modules:
  0.0 698.9 jit_solution(101815978232163255)
XLA Ops:
  9.0 4.0 convolution_convert_fusion
  18.7 26.0 %all-gather.9.cloned.1.call-done = bf16[1024,1024]{1,0:T(8,128)(2,1)} async-done(((bf16[128,1024]{1,0:T(8,128)(2,1)}), bf16[1024,1024]{1,0:T(8,128)(2,1)}) %all-gather.9.cloned.1.call-update) | async-done | bytes 2097168 | tf_op jit(solution)/shard_map/all_gather | solution.py:131
  48.6 26.5 %all-gather.11.cloned.1.call-done = bf16[1024,1024]{1,0:T(8,128)(2,1)} async-done(((bf16[128,1024]{1,0:T(8,128)(2,1)}), bf16[1024,1024]{1,0:T(8,128)(2,1)}) %all-gather.11.cloned.1.call-update) | async-done | bytes 2097168 | tf_op jit(solution)/shard_map/all_gather | solution.py:132
  79.1 13.9 %while.45 = (s32[]{:T(128)}, f32[1,16,128]{2,1,0:T(8,128)S(1)}, f32[1,16,128]{2,1,0:T(8,128)S(1)}, f32[1,16,128,64]{2,3,1,0:T(8,128)S(1)}, s32[2]{0:T(128)S(1)},...) while((s32[]{:T(128)}, f32[1,16,128]{2,1,0:T(8,128)S(1)}, ...), condition=%wide.region_9.10_spmd, body=%wide.region_3.9_spmd.sunk | while | flops 282544640 | bytes 20628860 | solution.py:52
  83.0 6.1 conditional.8
  98.3 4.9 fusion.92
  103.2 7.7 %fusion.60 = bf16[128,4096]{1,0:T(8,128)(2,1)S(1)} fusion(f32[128,4096]{1,0:T(8,128)S(1)} %fusion.92, bf16[4096,1024]{1,0:T(8,128)(2,1)} %param.27, bf16[1,128,1024]{2,1,0:T(8,128)(2,1)S(1)} %copy-done.18), kind=kOutput, calls=%fused_computation.80 | convolution fusion | flops 1084227584 | bytes 11796480 | tf_op jit(solution)/shard_map/dot_general | solution.py:62
  124.1 4.0 copy.73
  129.7 15.0 %all_gather.25 = bf16[1,1024,16]{1,2,0:T(8,128)(2,1)S(1)} all-gather(bf16[1,128,16]{1,2,0:T(8,128)(2,1)S(1)} %bitcast_convert_fusion), channel_id=1, replica_groups=mesh['dp'=4,'sq'=8] {'sq'}, dimensions={1}, use_global_device_ids=true | all-gather | bytes 36864 | tf_op jit(solution)/shard_map/all_gather | solution.py:253
  145.3 8.0 %all_gather.23 = bf16[1,1024,16]{1,2,0:T(8,128)(2,1)S(1)} all-gather(bf16[1,128,16]{1,2,0:T(8,128)(2,1)S(1)} %get-tuple-element.1073), channel_id=1, replica_groups=mesh['dp'=4,'sq'=8] {'sq'}, dimensions={1}, use_global_device_ids=true | all-gather | bytes 36864 | tf_op jit(solution)/shard_map/all_gather | solution.py:250
  155.3 20.4 %while.46 = (s32[]{:T(128)}, f32[1,16,128,64]{2,3,1,0:T(8,128)}, s32[2]{0:T(128)}, s32[128]{0:T(128)}, s32[1,8]{1,0:T(1,128)}, /*index=5*/s32[1,128]{1,0:T(1,128...) while((s32[]{:T(128)}, f32[1,16,128,64]{2,3,1,0:T(8,128)}, ...), condition=%wide.region_17.18_spmd, body=%wide.region_13.17_spmd.sunk | while | flops 409285120 | bytes 17499484 | solution.py:52
  159.7 11.6 %conditional.9 = (f32[1,16,128,64]{2,3,1,0:T(8,128)}) conditional(s32[]{:T(128)} %convert_element_type.291, f32[1,16,128,64]{2,3,1,0:T(8,128)} %get-tuple-element.1437, (s32[]{:T(128)}, s32[512]{0:T(512)S(1)}, s32[128]{0:T(128)}, s32[1,512,8]{1,2,0:T(8,128)S(1)}, s32[1,128]{1,0:T(1,128)}, /*index=5*/bf16[2,1,512,1024]{2,3,1,0:T(8,128)(2,1)}, ...), branch_computations={%region_14.14_spmd, %region_15.16_spmd} | conditional | flops 409276416 | bytes 17476628 | solution.py:192
  165.8 5.5 fusion.23
  177.5 4.0 copy.75
  182.4 36.2 %while.47 = (s32[]{:T(128)}, f32[1,16,128,64]{2,3,1,0:T(8,128)S(1)}, f32[1,16,128,64]{2,3,1,0:T(8,128)}, s32[2]{0:T(128)S(1)}, s32[]{:T(128)}, /*index=5*/s32[1,...) while((s32[]{:T(128)}, ...), condition=%wide.region_22.23_spmd.clone.clone, body=%wide.region_18.22_spmd.clone.clone.sunk | while | flops 547828352 | bytes 28265440 | solution.py:52
  184.5 16.3 %conditional.10 = ((f32[1,16,128,64]{2,3,1,0:T(8,128)S(1)}, f32[1,16,128,64]{2,3,1,0:T(8,128)})) conditional(s32[]{:T(128)} %convert_element_type.293, (f32[1,16,128,64]{2,3,1,0:T(8,128)S(1)}, f32[1,16,128,64]{2,3,1,0:T(8,128)}) %tuple.150, (s32[]{:T(128)}, s32[]{:T(128)}, s32[512]{0:T(512)S(1)}, s32[1,128]{1,0:T(1,128)S(1)}, ...), branch_computations={%region_19.19_spmd, %region_20.21_spmd} | conditional | flops 547819648 | bytes 28242020 | solution.py:243
  190.0 6.2 fusion.42
  196.2 4.5 fusion.43
  202.8 15.9 %conditional.10 = ((f32[1,16,128,64]{2,3,1,0:T(8,128)S(1)}, f32[1,16,128,64]{2,3,1,0:T(8,128)})) conditional(s32[]{:T(128)} %convert_element_type.293, (f32[1,16,128,64]{2,3,1,0:T(8,128)S(1)}, f32[1,16,128,64]{2,3,1,0:T(8,128)}) %tuple.150, (s32[]{:T(128)}, s32[]{:T(128)}, s32[512]{0:T(512)S(1)}, s32[1,128]{1,0:T(1,128)S(1)}, ...), branch_computations={%region_19.19_spmd, %region_20.21_spmd} | conditional | flops 547819648 | bytes 28242020 | solution.py:243
  208.3 6.2 fusion.42
  214.4 4.2 fusion.43
  219.8 7.5 %fusion.72 = f32[1024,3072]{1,0:T(8,128)} fusion(bf16[128,1024]{0,1:T(8,128)(2,1)S(1)} %bitcast.228, bf16[128,1024]{0,1:T(8,128)(2,1)S(1)} %bitcast.230, bf16[128,1024]{0,1:T(8,128)(2,1)} %bitcast.226, bf16[1,128,1024]{2,1,0:T(8,128)(2,1)S(1)} %copy-done.4, f32[1024]{0:T(1024)S(1)} %copy-done.30, f32[128]{0:T(128)S(1)} %copy-done.38), kind=kOutput, calls=%fused_computation.111 | convolution fusion | flops 808189952 | bytes 13636096 | tf_op jit(solution)/shard_map/dot_general | solution.py:56
  228.5 11.2 %fusion.91 = f32[1024,4096]{1,0:T(8,128)} fusion(bf16[128,4096]{1,0:T(8,128)(2,1)S(1)} %copy-done.9, f32[128,1024]{1,0:T(8,128)S(1)} %get-tuple-element.1089, f32[1024]{0:T(1024)S(1)} %copy-done.29, f32[128]{0:T(128)S(1)} %copy-done.35), kind=kOutput, calls=%fused_computation.140 | convolution fusion | flops 1074135040 | bytes 18354688 | tf_op jit(solution)/shard_map/dot_general | solution.py:56
  241.9 8.9 %fusion.74 = f32[4096,1024]{1,0:T(8,128)} fusion(bf16[1,128,1024]{2,1,0:T(8,128)(2,1)S(1)} %copy-done.19, f32[128,4096]{1,0:T(8,128)S(1)} %copy-done.3), kind=kOutput, calls=%fused_computation.113 | convolution fusion | flops 1078460416 | bytes 19136512 | tf_op jit(solution)/shard_map/dot_general | solution.py:56
  252.8 67.5 %reduce-scatter.5.cloned.1.call-done = f32[128,3072]{1,0:T(8,128)} async-done(((f32[1024,3072]{1,0:T(8,128)}), f32[128,3072]{1,0:T(8,128)}) %reduce-scatter.5.cloned.1.call-update) | async-done | bytes 1572880 | tf_op jit(solution)/shard_map/reduce_scatter | solution.py:276
  322.6 117.6 %reduce-scatter.9.cloned.1.call-done = f32[128,4096]{1,0:T(8,128)} async-done(((f32[1024,4096]{1,0:T(8,128)}), f32[128,4096]{1,0:T(8,128)}) %reduce-scatter.9.cloned.1.call-update) | async-done | bytes 2097168 | tf_op jit(solution)/shard_map/reduce_scatter | solution.py:279
  442.9 117.3 %reduce-scatter.11.cloned.1.call-done = f32[512,1024]{1,0:T(8,128)} async-done(((f32[4096,1024]{1,0:T(8,128)}), f32[512,1024]{1,0:T(8,128)}) %reduce-scatter.11.cloned.1.call-update) | async-done | bytes 2097168 | tf_op jit(solution)/shard_map/reduce_scatter | solution.py:280
  564.8 5.7 fusion.62
  570.6 5.2 fusion.66
  575.8 13.8 %all-reduce.2 = (bf16[1024]{0:T(1024)(128)(2,1)S(1)}, bf16[1024]{0:T(1024)(128)(2,1)S(1)}) all-reduce(f32[1024]{0:T(1024)S(1)} %get-tuple-element.989, f32[1024]{0:T(1024)S(1)} %copy-done.36), channel_id=6, replica_groups=mesh['dp'=4,'sq'=8] {'sq'}, use_global_device_ids=true, to_apply=%region_25.26.clone | all-reduce | flops 2048 | bytes 12288
  589.8 12.4 %all-reduce.3 = (bf16[128]{0:T(256)(128)(2,1)S(1)}, bf16[128]{0:T(256)(128)(2,1)S(1)}) all-reduce(bf16[128]{0:T(256)(128)(2,1)S(1)} %dynamic-slice.7, bf16[128]{0:T(256)(128)(2,1)S(1)} %dynamic-slice.6), channel_id=1, replica_groups=mesh['dp'=4,'sq'=8] {'dp'}, use_global_device_ids=true, to_apply=%region_26.27 | all-reduce | flops 256 | bytes 1024 | tf_op jit(solution)/shard_map/psum | solution.py:283
  604.2 81.7 %all-reduce.7.cloned.1.call-done = (bf16[128,3072]{1,0:T(8,128)(2,1)}, bf16[128,1024]{1,0:T(8,128)(2,1)}, bf16[128,4096]{1,0:T(8,128)(2,1)}, bf16[512,1024]{1,0:T(8,128)(2,1)}) async-done(((bf16[128,3072]{1,0:T(8,128)(2,1)}, bf16[128,1024]{1,0:T(8,128)(2,1)}, bf16[128,4096]{1,0:T(8,128)(2,1)}, bf16[512,1024]{1,0:T(8,128)(2,1)}), (bf16[128,3072]{1,0:T(8,128)(2,1)}, bf16[128,1024]{1,0:T(8,128)(2,1)}, ...) | async-done | bytes 3145744 | tf_op jit(solution)/shard_map/psum | solution.py:284
  (234 shorter events, 101.9 us)
Async XLA Ops:
  7.2 89.5 %copy-start = (bf16[1024,1024]{1,0:T(8,128)(2,1)S(1)}, bf16[1024,1024]{1,0:T(8,128)(2,1)}, u32[]{:S(2)}) copy-start(bf16[1024,1024]{1,0:T(8,128)(2,1)} %param.24) | copy-start | bytes 6291460
  7.2 37.5 %all-gather.9.cloned.1.call-start = ((), (), s32[]{:S(2)}) async-start(), calls=%async_computation.8 | async-start | bytes 2359296 | tf_op jit(solution)/shard_map/all_gather | solution.py:131
  13.0 4.1 copy-start.42
  14.0 61.1 %all-gather.11.cloned.1.call-start = ((), (), s32[]{:S(2)}) async-start(), calls=%async_computation.9 | async-start | bytes 2359296 | tf_op jit(solution)/shard_map/all_gather | solution.py:132
  14.7 109.4 %all-gather.13.cloned.1.call-start = ((), (), s32[]{:S(2)}) async-start(), calls=%async_computation.10 | async-start | bytes 2359296 | tf_op jit(solution)/shard_map/all_gather | solution.py:248
  15.4 162.1 %all-gather.15.cloned.1.call-start = ((), (), s32[]{:S(2)}) async-start(), calls=%async_computation.11 | async-start | bytes 2359296 | tf_op jit(solution)/shard_map/all_gather | solution.py:249
  92.9 5.3 copy-start.32
  98.2 16.3 %copy-start.34 = (f32[128]{0:T(128)}, f32[128]{0:T(128)S(1)}, u32[]{:S(2)}) copy-start(f32[128]{0:T(128)S(1)} %fusion.88) | copy-start | bytes 1540
  98.3 4.9 copy-start.18
  98.3 12.7 %slice-start = ((s8[8388608]{0:T(1024)(128)(4,1)}), s8[4194304]{0:T(1024)(128)(4,1)S(1)}, s32[]{:S(2)}) async-start(s8[8388608]{0:T(1024)(128)(4,1)} %bitcast.209), calls=%async_computation.13 | async-start | bytes 8388608
  103.2 7.8 %copy-start.2 = (f32[128,4096]{1,0:T(8,128)}, f32[128,4096]{1,0:T(8,128)S(1)}, u32[]{:S(2)}) copy-start(f32[128,4096]{1,0:T(8,128)S(1)} %fusion.92) | copy-start | bytes 6291460
  103.2 7.8 %slice-start.1 = ((s8[8388608]{0:T(1024)(128)(4,1)}), s8[4194304]{0:T(1024)(128)(4,1)S(1)}, s32[]{:S(2)}) async-start(s8[8388608]{0:T(1024)(128)(4,1)} %bitcast.209), calls=%async_computation.14 | async-start | bytes 8388608
  117.3 133.6 %reduce-scatter.7.cloned.1.call-start = ((), (), s32[]{:S(2)}) async-start(), calls=%async_computation.5 | async-start | bytes 4718592 | tf_op jit(solution)/shard_map/reduce_scatter | solution.py:277
  121.3 198.9 %reduce-scatter.5.cloned.1.call-start = ((), (), s32[]{:S(2)}) async-start(), calls=%async_computation.4 | async-start | bytes 14155776 | tf_op jit(solution)/shard_map/reduce_scatter | solution.py:276
  177.5 4.9 copy-start.27
  177.5 4.9 copy-start.33
  182.4 37.4 %copy-start.30 = (f32[1024]{0:T(1024)S(1)}, f32[1024]{0:T(1024)}, u32[]{:S(2)}) copy-start(f32[1024]{0:T(1024)} %param.22) | copy-start | bytes 12292
  182.4 37.4 %copy-start.38 = (f32[128]{0:T(128)S(1)}, f32[128]{0:T(128)}, u32[]{:S(2)}) copy-start(f32[128]{0:T(128)} %copy-done.37) | copy-start | bytes 1540
  196.2 4.5 copy-start.16
  214.4 4.2 copy-start.16
  219.7 7.6 %copy-start.23 = (bf16[1,16,128,64]{2,3,1,0:T(8,128)(2,1)}, bf16[1,16,128,64]{2,3,1,0:T(8,128)(2,1)S(1)}, u32[]{:S(2)}) copy-start(bf16[1,16,128,64]{2,3,1,0:T(8,128)(2,1)S(1)} %convert.20) | copy-start | bytes 786436
  219.8 7.5 %copy-start.25 = (bf16[1,16,128,64]{2,3,1,0:T(8,128)(2,1)}, bf16[1,16,128,64]{2,3,1,0:T(8,128)(2,1)S(1)}, u32[]{:S(2)}) copy-start(bf16[1,16,128,64]{2,3,1,0:T(8,128)(2,1)S(1)} %multiply_convert_fusion.2) | copy-start | bytes 786436
  227.3 212.8 %reduce-scatter.9.cloned.1.call-start = ((), (), s32[]{:S(2)}) async-start(), calls=%async_computation.6 | async-start | bytes 18874368 | tf_op jit(solution)/shard_map/reduce_scatter | solution.py:279
  239.7 320.4 %reduce-scatter.11.cloned.1.call-start = ((), (), s32[]{:S(2)}) async-start(), calls=%async_computation.7 | async-start | bytes 18874368 | tf_op jit(solution)/shard_map/reduce_scatter | solution.py:280
  250.9 435.0 %all-reduce.7.cloned.1.call-start = ((), (), s32[]{:S(2)}) async-start(), calls=%async_computation.12 | async-start | bytes 6291456 | tf_op jit(solution)/shard_map/psum | solution.py:284
  564.8 5.8 copy-start.22
  564.8 5.8 copy-start.24
  564.8 5.8 copy-start.26
  564.8 5.8 copy-start.39
  570.6 5.2 copy-start.36
  570.6 32.6 %copy-start.41 = (f32[128]{0:T(128)S(1)}, f32[128]{0:T(128)}, u32[]{:S(2)}) copy-start(f32[128]{0:T(128)} %copy-done.40) | copy-start | bytes 1540
  570.6 32.6 %copy-start.6 = (f32[128,1024]{1,0:T(8,128)S(1)}, f32[128,1024]{1,0:T(8,128)}, u32[]{:S(2)}) copy-start(f32[128,1024]{1,0:T(8,128)} %copy-done.5) | copy-start | bytes 1572868
  (25 other events, 47.7 us)
Sparse Core Ops, SparseCore 0:
  14.1 30.5 all-gather.8
  47.2 27.8 all-gather.10
  77.0 27.8 all-gather.12
  117.5 34.1 all-gather.14
  154.8 51.3 reduce-scatter.6
  227.5 92.7 reduce-scatter.4
  324.2 115.9 reduce-scatter.8
  444.2 115.9 reduce-scatter.10
  563.5 122.3 all-reduce.6
where the time goes:
time: 700 us; the launch traced here: 699 us
  waiting for transfers between devices  438 us (63%)
  matrix products  103 us (15%)
  local copies, waits for them, and re-layouts  50.6 us (7%)
  blocking collectives  49.2 us (7%)
  other arithmetic  35.8 us (5%)
  between operations  15 us (2%)
    reduce_scatter x1, waiting for transfers between devices, shards(): lax.psum_scatter(grad_up, 'sq', scatter_dimension=0, tiled=True)  118 us
    reduce_scatter x1, waiting for transfers between devices, shards(): lax.psum_scatter(grad_down, 'sq', scatter_dimension=0, tiled=True)  117 us
    psum x1, waiting for transfers between devices, shards(): lax.psum(shares_sq[1].astype(jnp.bfloat16), 'dp').astype(jnp.float32)  81.7 us
    reduce_scatter x1, waiting for transfers between devices, shards(): lax.psum_scatter(grad_qkv, 'sq', scatter_dimension=0, tiled=True)  67.5 us
    dot_general x4, matrix products, contract_rows(): lax.dot_general(left, right, (((0,), (0,)), ((), ())), preferred_element_...  31.4 us
    all_gather x1, waiting for transfers between devices, shards(): lax.all_gather(value_rows, 'sq', axis=1, tiled=True)  26.5 us
    all_gather x1, waiting for transfers between devices, shards(): lax.all_gather(key_rows, 'sq', axis=1, tiled=True)  26 us
    dot_general x4, matrix products, times_transpose(): lax.dot_general(left, right, (((1,), (1,)), ((), ())), preferred_element_...  18.2 us
  transfers between devices with their start and end apart: 9, of which 6 were waited for; matrix products, arithmetic and copies ran while one was open for 24% of the time, Pallas kernels for 0%

commit v1 on v0

--- a/solution.py
+++ b/solution.py
@@ -281,7 +281,9 @@
     )
     totals = (
         lax.psum(shares_sq[0].astype(jnp.bfloat16), "dp").astype(jnp.float32),
-        lax.psum(shares_sq[1].astype(jnp.bfloat16), "dp").astype(jnp.float32),
+        jnp.sum(lax.all_gather(shares_sq[1].astype(jnp.bfloat16), "dp"), axis=0).astype(
+            jnp.float32
+        ),
         lax.psum(shares_sq[2].astype(jnp.bfloat16), "dp").astype(jnp.float32),
         lax.psum(shares_sq[3].astype(jnp.bfloat16), "dp").astype(jnp.float32),
         lax.psum(shares_sq[4].astype(jnp.bfloat16), "dp").astype(jnp.float32),

time: 700 us -> 794 us (1.13)
  waiting for transfers between devices: 438 us -> 522 us
    reduce_scatter x1, waiting for transfers between devices: 0.02 us -> 52.1 us  [shards(): lax.psum_scatter(grad_outproj, 'sq', scatter_dimension=0, tiled=True)]
    all_gather x0 -> x1, waiting for transfers between devices: none -> 22.6 us  [shards(): lax.all_gather(shares_sq[1].astype(jnp.bfloat16), 'dp')]
    psum x1, waiting for transfers between devices: 81.7 us -> 94.4 us  [shards(): lax.psum(shares_sq[2].astype(jnp.bfloat16), 'dp').astype(jnp.float32)]
    unnamed x94 -> x84, local copies, waits for them, and re-layouts: 17.1 us -> 15.4 us
  transfers between devices with their start and end apart: 9 -> 10, of which waited for: 6 -> 8; matrix products, arithmetic and copies ran while one was open for 24% -> 16% of each run, Pallas kernels for 0% -> 0%
where the time goes in v1:
time: 794 us; the launch traced here: 787 us
  waiting for transfers between devices  522 us (66%)
  matrix products  103 us (13%)
  local copies, waits for them, and re-layouts  49.3 us (6%)
  blocking collectives  48.7 us (6%)
  other arithmetic  40.8 us (5%)
  between operations  15.5 us (2%)
    reduce_scatter x1, waiting for transfers between devices, shards(): lax.psum_scatter(grad_down, 'sq', scatter_dimension=0, tiled=True)  118 us
    reduce_scatter x1, waiting for transfers between devices, shards(): lax.psum_scatter(grad_up, 'sq', scatter_dimension=0, tiled=True)  117 us
    psum x1, waiting for transfers between devices, shards(): lax.psum(shares_sq[2].astype(jnp.bfloat16), 'dp').astype(jnp.float32)  94.4 us
    reduce_scatter x1, waiting for transfers between devices, shards(): lax.psum_scatter(grad_qkv, 'sq', scatter_dimension=0, tiled=True)  64.4 us
    reduce_scatter x1, waiting for transfers between devices, shards(): lax.psum_scatter(grad_outproj, 'sq', scatter_dimension=0, tiled=True)  52.1 us
    dot_general x4, matrix products, contract_rows(): lax.dot_general(left, right, (((0,), (0,)), ((), ())), preferred_element_...  32 us
    all_gather x1, waiting for transfers between devices, shards(): lax.all_gather(key_rows, 'sq', axis=1, tiled=True)  25.9 us
    all_gather x1, waiting for transfers between devices, shards(): lax.all_gather(value_rows, 'sq', axis=1, tiled=True)  25.5 us
  transfers between devices with their start and end apart: 10, of which 8 were waited for; matrix products, arithmetic and copies ran while one was open for 16% of the time, Pallas kernels for 0%

profile of v1, /device:TPU:0, one launch (start us, length us, event | category | flops | bytes accessed | tf_op | source)
XLA Modules:
  0.0 787.5 jit_solution(16129449635495804369)
XLA Ops:
  19.1 25.5 %all-gather.13.cloned.1.call-done = bf16[1024,1024]{1,0:T(8,128)(2,1)} async-done(((bf16[128,1024]{1,0:T(8,128)(2,1)}), bf16[1024,1024]{1,0:T(8,128)(2,1)}) %all-gather.13.cloned.1.call-update) | async-done | bytes 2097168 | tf_op jit(solution)/shard_map/all_gather | solution.py:132
  48.5 25.9 %all-gather.11.cloned.1.call-done = bf16[1024,1024]{1,0:T(8,128)(2,1)} async-done(((bf16[128,1024]{1,0:T(8,128)(2,1)}), bf16[1024,1024]{1,0:T(8,128)(2,1)}) %all-gather.11.cloned.1.call-update) | async-done | bytes 2097168 | tf_op jit(solution)/shard_map/all_gather | solution.py:131
  78.4 14.2 %while.45 = (s32[]{:T(128)}, f32[1,16,128]{2,1,0:T(8,128)S(1)}, f32[1,16,128]{2,1,0:T(8,128)S(1)}, f32[1,16,128,64]{2,3,1,0:T(8,128)S(1)}, s32[2]{0:T(128)S(1)},...) while((s32[]{:T(128)}, f32[1,16,128]{2,1,0:T(8,128)S(1)}, ...), condition=%wide.region_9.10_spmd, body=%wide.region_3.9_spmd.sunk | while | flops 282544640 | bytes 20628860 | solution.py:52
  82.2 6.1 conditional.8
  98.0 4.9 fusion.92
  103.0 7.7 fusion.60
  120.9 4.0 copy.73
  125.5 14.8 %all_gather.29 = bf16[1,1024,16]{1,2,0:T(8,128)(2,1)S(1)} all-gather(bf16[1,128,16]{1,2,0:T(8,128)(2,1)S(1)} %get-tuple-element.1072), channel_id=1, replica_groups=mesh['dp'=4,'sq'=8] {'sq'}, dimensions={1}, use_global_device_ids=true | all-gather | bytes 36864 | tf_op jit(solution)/shard_map/all_gather | solution.py:250
  141.9 8.0 %all_gather.31 = bf16[1,1024,16]{1,2,0:T(8,128)(2,1)S(1)} all-gather(bf16[1,128,16]{1,2,0:T(8,128)(2,1)S(1)} %bitcast_convert_fusion), channel_id=1, replica_groups=mesh['dp'=4,'sq'=8] {'sq'}, dimensions={1}, use_global_device_ids=true | all-gather | bytes 36864 | tf_op jit(solution)/shard_map/all_gather | solution.py:253
  152.0 19.8 %while.46 = (s32[]{:T(128)}, f32[1,16,128,64]{2,3,1,0:T(8,128)}, s32[2]{0:T(128)}, s32[128]{0:T(128)}, s32[1,8]{1,0:T(1,128)}, /*index=5*/s32[1,128]{1,0:T(1,128...) while((s32[]{:T(128)}, f32[1,16,128,64]{2,3,1,0:T(8,128)}, ...), condition=%wide.region_17.18_spmd, body=%wide.region_13.17_spmd.sunk | while | flops 409285120 | bytes 17499484 | solution.py:52
  156.7 10.4 %conditional.9 = (f32[1,16,128,64]{2,3,1,0:T(8,128)}) conditional(s32[]{:T(128)} %convert_element_type.293, f32[1,16,128,64]{2,3,1,0:T(8,128)} %get-tuple-element.1436, (s32[]{:T(128)}, s32[512]{0:T(512)S(1)}, s32[128]{0:T(128)}, s32[1,512,8]{1,2,0:T(8,128)S(1)}, s32[1,128]{1,0:T(1,128)}, /*index=5*/bf16[2,1,512,1024]{2,3,1,0:T(8,128)(2,1)}, ...), branch_computations={%region_14.14_spmd, %region_15.16_spmd} | conditional | flops 409276416 | bytes 17476628 | solution.py:192
  162.1 5.1 fusion.23
  178.5 35.8 %while.47 = (s32[]{:T(128)}, f32[1,16,128,64]{2,3,1,0:T(8,128)S(1)}, f32[1,16,128,64]{2,3,1,0:T(8,128)}, s32[2]{0:T(128)S(1)}, s32[]{:T(128)}, /*index=5*/s32[1,...) while((s32[]{:T(128)}, ...), condition=%wide.region_22.23_spmd.clone.clone, body=%wide.region_18.22_spmd.clone.clone.sunk | while | flops 547828352 | bytes 28265440 | solution.py:52
  180.6 15.7 %conditional.10 = ((f32[1,16,128,64]{2,3,1,0:T(8,128)S(1)}, f32[1,16,128,64]{2,3,1,0:T(8,128)})) conditional(s32[]{:T(128)} %convert_element_type.295, (f32[1,16,128,64]{2,3,1,0:T(8,128)S(1)}, f32[1,16,128,64]{2,3,1,0:T(8,128)}) %tuple.150, (s32[]{:T(128)}, s32[]{:T(128)}, s32[512]{0:T(512)S(1)}, s32[1,128]{1,0:T(1,128)}, ...), branch_computations={%region_19.19_spmd, %region_20.21_spmd} | conditional | flops 547819648 | bytes 28242020 | solution.py:243
  186.0 6.1 fusion.42
  192.2 4.2 fusion.43
  198.5 15.7 %conditional.10 = ((f32[1,16,128,64]{2,3,1,0:T(8,128)S(1)}, f32[1,16,128,64]{2,3,1,0:T(8,128)})) conditional(s32[]{:T(128)} %convert_element_type.295, (f32[1,16,128,64]{2,3,1,0:T(8,128)S(1)}, f32[1,16,128,64]{2,3,1,0:T(8,128)}) %tuple.150, (s32[]{:T(128)}, s32[]{:T(128)}, s32[512]{0:T(512)S(1)}, s32[1,128]{1,0:T(1,128)}, ...), branch_computations={%region_19.19_spmd, %region_20.21_spmd} | conditional | flops 547819648 | bytes 28242020 | solution.py:243
  203.9 6.1 fusion.42
  210.0 4.2 fusion.43
  215.4 7.4 fusion.72
  228.4 12.4 %fusion.74 = f32[4096,1024]{1,0:T(8,128)} fusion(bf16[1,128,1024]{2,1,0:T(8,128)(2,1)S(1)} %copy-done.18, f32[128,4096]{1,0:T(8,128)S(1)} %copy-done.3), kind=kOutput, calls=%fused_computation.113 | convolution fusion | flops 1078460416 | bytes 19136512 | tf_op jit(solution)/shard_map/dot_general | solution.py:56
  241.5 9.5 %fusion.91 = f32[1024,4096]{1,0:T(8,128)} fusion(bf16[128,4096]{1,0:T(8,128)(2,1)} %copy-done.10, f32[128,1024]{1,0:T(8,128)S(1)} %get-tuple-element.1088, f32[1024]{0:T(1024)S(1)} %copy-done.27, f32[128]{0:T(128)S(1)} %copy-done.30), kind=kOutput, calls=%fused_computation.140 | convolution fusion | flops 1074135040 | bytes 18354688 | tf_op jit(solution)/shard_map/dot_general | solution.py:56
  251.0 64.4 %reduce-scatter.5.cloned.1.call-done = f32[128,3072]{1,0:T(8,128)} async-done(((f32[1024,3072]{1,0:T(8,128)}), f32[128,3072]{1,0:T(8,128)}) %reduce-scatter.5.cloned.1.call-update) | async-done | bytes 1572880 | tf_op jit(solution)/shard_map/reduce_scatter | solution.py:276
  317.9 52.1 %reduce-scatter.7.cloned.1.call-done = f32[128,1024]{1,0:T(8,128)} async-done(((f32[1024,1024]{1,0:T(8,128)}), f32[128,1024]{1,0:T(8,128)}) %reduce-scatter.7.cloned.1.call-update) | async-done | bytes 524304 | tf_op jit(solution)/shard_map/reduce_scatter | solution.py:277
  371.8 118.2 %reduce-scatter.11.cloned.1.call-done = f32[512,1024]{1,0:T(8,128)} async-done(((f32[4096,1024]{1,0:T(8,128)}), f32[512,1024]{1,0:T(8,128)}) %reduce-scatter.11.cloned.1.call-update) | async-done | bytes 2097168 | tf_op jit(solution)/shard_map/reduce_scatter | solution.py:280
  492.7 117.2 %reduce-scatter.9.cloned.1.call-done = f32[128,4096]{1,0:T(8,128)} async-done(((f32[1024,4096]{1,0:T(8,128)}), f32[128,4096]{1,0:T(8,128)}) %reduce-scatter.9.cloned.1.call-update) | async-done | bytes 2097168 | tf_op jit(solution)/shard_map/reduce_scatter | solution.py:279
  613.9 5.7 fusion.62
  619.6 5.5 fusion.66
  625.2 13.8 %all-reduce.2 = (bf16[1024]{0:T(1024)(128)(2,1)S(1)}, bf16[1024]{0:T(1024)(128)(2,1)S(1)}) all-reduce(f32[1024]{0:T(1024)S(1)} %get-tuple-element.989, f32[1024]{0:T(1024)S(1)} %copy-done.31), channel_id=7, replica_groups=mesh['dp'=4,'sq'=8] {'sq'}, use_global_device_ids=true, to_apply=%region_25.26.clone | all-reduce | flops 2048 | bytes 12288
  639.1 12.0 %all-reduce.3 = (bf16[128]{0:T(256)(128)(2,1)S(1)}, bf16[128]{0:T(256)(128)(2,1)S(1)}) all-reduce(bf16[128]{0:T(256)(128)(2,1)S(1)} %dynamic-slice.7, bf16[128]{0:T(256)(128)(2,1)S(1)} %dynamic-slice.6), channel_id=1, replica_groups=mesh['dp'=4,'sq'=8] {'dp'}, use_global_device_ids=true, to_apply=%region_26.27 | all-reduce | flops 256 | bytes 1024 | tf_op jit(solution)/shard_map/psum | solution.py:283
  653.2 22.6 %all-gather.19.cloned.1.call-done = bf16[512,3072]{1,0:T(8,128)(2,1)} async-done(((bf16[128,3072]{1,0:T(8,128)(2,1)}), bf16[512,3072]{1,0:T(8,128)(2,1)}) %all-gather.19.cloned.1.call-update) | async-done | bytes 3145744 | tf_op jit(solution)/shard_map/all_gather | solution.py:284
  679.6 94.4 %all-reduce.7.cloned.1.call-done = (bf16[128,1024]{1,0:T(8,128)(2,1)}, bf16[128,4096]{1,0:T(8,128)(2,1)}, bf16[512,1024]{1,0:T(8,128)(2,1)}) async-done(((bf16[128,1024]{1,0:T(8,128)(2,1)}, bf16[128,4096]{1,0:T(8,128)(2,1)}, bf16[512,1024]{1,0:T(8,128)(2,1)}), (bf16[128,1024]{1,0:T(8,128)(2,1)}, bf16[128,4096]{1,0:T(8,128)(2,1)}, bf16[512,1024]{1,0:T(8,128)(2,1)})) %all-reduce.7.cloned.1.call-update) | async-done | bytes 2359312 | tf_op jit(solution)/shard_map/psum | solution.py:287
  (228 shorter events, 112.4 us)
Async XLA Ops:
  7.2 89.2 %copy-start = (bf16[1024,1024]{1,0:T(8,128)(2,1)S(1)}, bf16[1024,1024]{1,0:T(8,128)(2,1)}, u32[]{:S(2)}) copy-start(bf16[1024,1024]{1,0:T(8,128)(2,1)} %param.24) | copy-start | bytes 6291460
  7.2 37.4 %all-gather.13.cloned.1.call-start = ((), (), s32[]{:S(2)}) async-start(), calls=%async_computation.9 | async-start | bytes 2359296 | tf_op jit(solution)/shard_map/all_gather | solution.py:132
  13.9 60.6 %all-gather.11.cloned.1.call-start = ((), (), s32[]{:S(2)}) async-start(), calls=%async_computation.8 | async-start | bytes 2359296 | tf_op jit(solution)/shard_map/all_gather | solution.py:131
  14.6 106.3 %all-gather.15.cloned.1.call-start = ((), (), s32[]{:S(2)}) async-start(), calls=%async_computation.10 | async-start | bytes 2359296 | tf_op jit(solution)/shard_map/all_gather | solution.py:248
  15.3 158.2 %all-gather.17.cloned.1.call-start = ((), (), s32[]{:S(2)}) async-start(), calls=%async_computation.11 | async-start | bytes 2359296 | tf_op jit(solution)/shard_map/all_gather | solution.py:249
  97.9 16.3 %copy-start.29 = (f32[128]{0:T(128)}, f32[128]{0:T(128)S(1)}, u32[]{:S(2)}) copy-start(f32[128]{0:T(128)S(1)} %fusion.88) | copy-start | bytes 1540
  98.0 5.0 copy-start.17
  98.0 12.7 %slice-start = ((s8[8388608]{0:T(1024)(128)(4,1)}), s8[4194304]{0:T(1024)(128)(4,1)S(1)}, s32[]{:S(2)}) async-start(s8[8388608]{0:T(1024)(128)(4,1)} %bitcast.210), calls=%async_computation.14 | async-start | bytes 8388608
  102.9 7.8 copy-start.2
  102.9 7.8 slice-start.1
  117.1 198.4 %reduce-scatter.5.cloned.1.call-start = ((), (), s32[]{:S(2)}) async-start(), calls=%async_computation.4 | async-start | bytes 14155776 | tf_op jit(solution)/shard_map/reduce_scatter | solution.py:276
  120.9 19.4 %copy-start.12 = (f32[128,1024]{1,0:T(8,128)S(1)}, f32[128,1024]{1,0:T(8,128)}, u32[]{:S(2)}) copy-start(f32[128,1024]{1,0:T(8,128)} %get-tuple-element.1090) | copy-start | bytes 1572868
  173.6 4.9 copy-start.25
  178.4 37.0 %copy-start.28 = (f32[1024]{0:T(1024)S(1)}, f32[1024]{0:T(1024)}, u32[]{:S(2)}) copy-start(f32[1024]{0:T(1024)} %param.22) | copy-start | bytes 12292
  178.5 37.0 %copy-start.33 = (f32[128]{0:T(128)S(1)}, f32[128]{0:T(128)}, u32[]{:S(2)}) copy-start(f32[128]{0:T(128)} %copy-done.32) | copy-start | bytes 1540
  215.3 7.5 copy-start.21
  215.4 7.5 copy-start.23
  222.9 147.1 %reduce-scatter.7.cloned.1.call-start = ((), (), s32[]{:S(2)}) async-start(), calls=%async_computation.5 | async-start | bytes 4718592 | tf_op jit(solution)/shard_map/reduce_scatter | solution.py:277
  226.8 263.2 %reduce-scatter.11.cloned.1.call-start = ((), (), s32[]{:S(2)}) async-start(), calls=%async_computation.7 | async-start | bytes 18874368 | tf_op jit(solution)/shard_map/reduce_scatter | solution.py:280
  240.8 369.0 %reduce-scatter.9.cloned.1.call-start = ((), (), s32[]{:S(2)}) async-start(), calls=%async_computation.6 | async-start | bytes 18874368 | tf_op jit(solution)/shard_map/reduce_scatter | solution.py:279
  251.0 424.8 %all-gather.19.cloned.1.call-start = ((), (), s32[]{:S(2)}) async-start(), calls=%async_computation.12 | async-start | bytes 3932160 | tf_op jit(solution)/shard_map/all_gather | solution.py:284
  317.8 456.2 %all-reduce.7.cloned.1.call-start = ((), (), s32[]{:S(2)}) async-start(), calls=%async_computation.13 | async-start | bytes 4718592 | tf_op jit(solution)/shard_map/psum | solution.py:287
  492.7 119.9 %copy-start.38 = (u32[32]{0:T(128)S(1)}, u32[32]{0:T(128)}, u32[]{:S(2)}) copy-start(u32[32]{0:T(128)} %constant.168) | copy-start | bytes 388
  613.9 5.7 copy-start.20
  613.9 5.7 copy-start.22
  613.9 5.7 copy-start.24
  613.9 5.7 copy-start.34
  619.6 5.5 copy-start.31
  619.6 32.6 %copy-start.36 = (f32[128]{0:T(128)S(1)}, f32[128]{0:T(128)}, u32[]{:S(2)}) copy-start(f32[128]{0:T(128)} %copy-done.35) | copy-start | bytes 1540
  619.6 32.6 %copy-start.7 = (f32[128,1024]{1,0:T(8,128)S(1)}, f32[128,1024]{1,0:T(8,128)}, u32[]{:S(2)}) copy-start(f32[128,1024]{1,0:T(8,128)} %copy-done.5) | copy-start | bytes 1572868
  774.1 4.8 copy-start.19
  775.9 4.5 copy-start.1
  (21 other events, 40.2 us)
Sparse Core Ops, SparseCore 0:
  14.0 30.5 all-gather.12
  46.5 27.8 all-gather.10
  76.3 27.8 all-gather.14
  117.2 34.0 all-gather.16
  223.0 92.3 reduce-scatter.4
  318.6 51.3 reduce-scatter.6
  374.0 115.9 reduce-scatter.10
  493.9 115.9 reduce-scatter.8
  612.1 63.6 all-gather.18
  679.0 95.0 all-reduce.6
